TPU v7x, 1024 devices: a whole 4x4x32 slice. The times are simulated.
1024 devices in a mesh: gx: 16 (over z_lo, core), gy: 16 (over y, z_hi), gz: 4 (over x).
Axes of the slice: x: 4, y: 4, z: 32 (z_hi: 4, z_lo: 8; z = z_hi * 8 + z_lo), core: 2. Of those that a mesh axis runs over, the one named last changes fastest.
Arguments:
- fine_multipoles: bfloat16 [64, 64, 32, 64], P('gx', 'gy', 'gz'), may hold values from -6 to 6
- fine_translations: bfloat16 [158, 64, 64], replicated, may hold values from -0.0546875 to 0.0546875
- coarse_multipoles: bfloat16 [64, 64, 16, 64], P('gx', 'gy', 'gz'), may hold values from -6 to 6
- coarse_translations: bfloat16 [158, 64, 64], replicated, may hold values from -0.0546875 to 0.0546875
Outputs:
- fine_locals: float32 [64, 64, 32, 64], P('gx', 'gy', 'gz')
- coarse_locals: float32 [64, 64, 16, 64], P('gx', 'gy', 'gz')
All inputs are finite; a program needn't handle non-finite values.
Results may differ from a plain program's by a relative error of at most 0.00045.
Values may be sent and summed in bfloat16 or wider, within the bound.
A program may use at most 128 MiB of HBM per device.

v0:
```python
import functools

import jax
import jax.numpy as jnp
import numpy as np
from jax import lax
from jax.experimental import pallas as pl
from jax.experimental.pallas import tpu as pltpu
from jax.sharding import PartitionSpec as P

MESH = pl.DeviceIdType.MESH
BF16 = jnp.bfloat16
F32 = jnp.float32

GROUPS = [(0, ey) for ey in range(4)] + [(ex, ey) for ex in range(1, 4) for ey in range(-3, 4)]
PLACES = 7 * len(GROUPS)
Y_PAIRS = ((-3, -2), (-1, 0), (1, 2), (3,))
PLANE = [(sx, sz) for sx in (-1, 0, 1) for sz in (-1, 0, 1) if (sx, sz) != (0, 0)]
FINE_SLOTS = (0, 2, 4, 5, 6, 8)
COARSE_SLOTS = (1, 3, 7, 9)
SLOTS = 10


def group(ex, ey):
    return ey if ex == 0 else 4 + (ex - 1) * 7 + ey + 3


def half_offsets():
    listed = []
    for step_x in range(-3, 4):
        for step_y in range(-3, 4):
            for step_z in range(-3, 4):
                if max(abs(step_x), abs(step_y), abs(step_z)) < 2:
                    continue
                if step_x > 0 or (step_x == 0 and (step_y > 0 or (step_y == 0 and step_z > 0))):
                    listed.append((step_x, step_y, step_z))
    return listed


def table_runs():
    places = [group(x, y) * 7 + z + 3 for x, y, z in half_offsets()]
    runs = []
    for index, place in enumerate(places):
        cut = place in (4 * 7, 11 * 7, 18 * 7)
        if runs and runs[-1][1] + runs[-1][2] == place and not cut:
            runs[-1][2] += 1
        else:
            runs.append([index, place, 1])
    empty = [place for place in range(PLACES) if place not in set(places)]
    return [tuple(run) for run in runs], empty


RUNS, EMPTY = table_runs()


def pack_level(src, stage, own, up, down, nz, base, msg_base):
    zp = nz // 2
    stage[0 : 16 * nz, 0:64] = src[...].astype(F32).reshape(16 * nz, 64)
    for x in range(4):
        for y in range(4):
            row = (x * 4 + y) * nz
            even = stage[pl.ds(row, zp, stride=2), 0:64]
            odd = stage[pl.ds(row + 1, zp, stride=2), 0:64]
            both = jnp.concatenate([even, odd], axis=1)
            tile = (x // 2) * zp * 2 + x % 2
            own[pl.ds(base + tile * 8 + 2 + y, zp, stride=16), :] = both
            face = up if y >= 2 else down
            face[pl.ds(msg_base + tile * 2 + y % 2, zp, stride=4), :] = both


def unpack_level(dst, tiles, nz):
    zp = nz // 2
    for x in range(4):
        for y in range(4):
            start = ((x // 2) * zp * 2 + x % 2) * 8 + y
            both = tiles[pl.ds(start, zp, stride=16), :]
            dst[x, y, pl.ds(0, zp, stride=2), :] = both[:, 0:64]
            dst[x, y, pl.ds(1, zp, stride=2), :] = both[:, 64:128]


def build_weights(places, ahead, behind, first, last):
    @pl.loop(first, last)
    def _(g):
        blocks = [places[g * 7 + e] for e in range(7)]
        for j in range(6):
            pair = jnp.concatenate([blocks[j], blocks[j + 1]], axis=1)
            half = 64 if j % 2 == 0 else 0
            ahead[g, half : half + 64, (j // 2) * 128 : (j // 2) * 128 + 128] = pair
            behind[g, (5 - j) * 64 : (5 - j) * 64 + 64, :] = pair


def shift_tiles(halo, odd, high, low):
    zero = jnp.zeros((8, 128), F32)

    @pl.loop(0, SLOTS)
    def _(s):
        wide = [halo[q, s].astype(F32) for q in range(4)]
        for q in range(3):
            odd[q, s] = jnp.concatenate([wide[q][8:16], wide[q + 1][0:8]], axis=0).astype(BF16)
        for q in range(2):
            high[q, s] = jnp.concatenate([wide[q + 2][8:16], zero], axis=0).astype(BF16)
            low[q, s] = jnp.concatenate([zero, wide[q][0:8]], axis=0).astype(BF16)


def sources(halo, odd, high, low, dx, slots):
    if dx % 2 == 0:
        part, first = halo, 1 + dx // 2
    elif dx == 3:
        part, first = high, 0
    elif dx == -3:
        part, first = low, 0
    else:
        part, first = odd, (dx + 1) // 2
    zp = len(slots) - 2
    columns = []
    for step in range(3):
        columns.append(
            jnp.concatenate([part[first + q, slots[z + step]] for q in range(2) for z in range(zp)], axis=0)
        )
    return jnp.concatenate(columns, axis=1)


def dot_ahead(left, weights):
    return lax.dot_general(left, weights, (((1,), (1,)), ((), ())), preferred_element_type=F32)


def dot_behind(left, weights):
    return lax.dot_general(left, weights, (((1,), (0,)), ((), ())), preferred_element_type=F32)


def level(halo, odd, high, low, ahead, behind, slots):
    get = functools.partial(sources, halo, odd, high, low, slots=slots)
    forward = {x: get(x) for x in range(0, 4)}
    backward = {x: get(-x) for x in range(0, 4)}
    rows = forward[0].shape[0]
    y = lax.broadcasted_iota(jnp.int32, (rows // 8, 8, 128), 1)
    total = None
    for pair in Y_PAIRS:
        xs = range(0, 4) if min(pair) >= 0 else range(1, 4)
        left = jnp.concatenate([forward[x] for x in xs], axis=1)
        right = jnp.concatenate(
            [jnp.concatenate([ahead[group(x, ey)] for x in xs], axis=1) for ey in pair], axis=0
        )
        sums = dot_ahead(left, right)
        xs = range(0, 4) if max(pair) <= 0 else range(1, 4)
        left = jnp.concatenate([backward[x] for x in xs], axis=1)
        right = jnp.concatenate(
            [jnp.concatenate([behind[group(x, -ey)] for x in xs], axis=0) for ey in pair], axis=1
        )
        sums = sums + dot_behind(left, right)
        for place, ey in enumerate(pair):
            term = sums[:, place * 128 : place * 128 + 128]
            if ey == 0:
                term = term + dot_ahead(forward[0], ahead[group(0, 0)])
            term = term.reshape(rows // 8, 8, 128)
            term = pltpu.roll(term, (-(2 + ey)) % 8, 1)
            if ey == 3:
                term = jnp.where(y % 2 == 0, term, 0.0)
            if ey == -3:
                term = jnp.where(y % 2 == 1, term, 0.0)
            total = term if total is None else total + term
    return total.reshape(rows, 128)


def kernel(
    sizes, fine, fine_table, coarse, coarse_table, fine_out, coarse_out,
    fine_places, coarse_places, fine_ahead, fine_behind, coarse_ahead, coarse_behind,
    halo, odd, high, low, stage, own, faces, sent, got, spread, tiles,
    table_sem, y_send, y_recv, plane_send, plane_recv,
):
    nx, ny, nz = sizes
    gx, gy, gz = lax.axis_index("gx"), lax.axis_index("gy"), lax.axis_index("gz")

    copies = []
    for at, (table, places) in enumerate(((fine_table, fine_places), (coarse_table, coarse_places))):
        copies.append([
            pltpu.make_async_copy(
                table.at[pl.ds(c, n)], places.at[pl.ds(p, n)], table_sem.at[at, k]
            )
            for k, (c, p, n) in enumerate(RUNS)
        ])
    for some in copies:
        for copy in some:
            copy.start()

    @pl.when(gx == 0)
    def _():
        halo[0] = jnp.zeros((SLOTS, 16, 128), BF16)

    @pl.when(gx == nx - 1)
    def _():
        halo[3] = jnp.zeros((SLOTS, 16, 128), BF16)

    @pl.when(gz == 0)
    def _():
        halo[:, 0:2] = jnp.zeros((4, 2, 16, 128), BF16)

    @pl.when(gz == nz - 1)
    def _():
        halo[:, 8:10] = jnp.zeros((4, 2, 16, 128), BF16)

    @pl.when(gy == 0)
    def _():
        got[0] = jnp.zeros((48, 128), BF16)

    @pl.when(gy == ny - 1)
    def _():
        got[1] = jnp.zeros((48, 128), BF16)

    def in_y(sy):
        return (gy + sy >= 0) & (gy + sy < ny)

    def in_plane(sx, sz):
        return (gx + sx >= 0) & (gx + sx < nx) & (gz + sz >= 0) & (gz + sz < nz)

    def at_y(sy):
        return (gx, lax.rem(gy + sy + ny, ny), gz)

    def at_plane(sx, sz):
        return (lax.rem(gx + sx + nx, nx), gy, lax.rem(gz + sz + nz, nz))

    barrier = pltpu.get_barrier_semaphore()
    neighbours = jnp.int32(0)
    for sy in (1, -1):
        neighbours += in_y(sy).astype(jnp.int32)

        @pl.when(in_y(sy))
        def _():
            pl.semaphore_signal(barrier, inc=1, device_id=at_y(sy), device_id_type=MESH)

    for sx, sz in PLANE:
        neighbours += in_plane(sx, sz).astype(jnp.int32)

        @pl.when(in_plane(sx, sz))
        def _():
            pl.semaphore_signal(barrier, inc=1, device_id=at_plane(sx, sz), device_id_type=MESH)

    pack_level(fine, stage, own, faces.at[0], faces.at[1], 8, 0, 0)
    pack_level(coarse, stage, own, faces.at[0], faces.at[1], 4, 128, 32)
    sent[...] = faces[...].astype(BF16)

    y_copies = [
        (sy, -sy, pltpu.make_async_remote_copy(
            src_ref=sent.at[k], dst_ref=got.at[k], send_sem=y_send.at[k], recv_sem=y_recv.at[k],
            device_id=at_y(sy), device_id_type=MESH,
        ))
        for k, sy in enumerate((1, -1))
    ]
    pl.semaphore_wait(barrier, neighbours)
    for to, _, copy in y_copies:

        @pl.when(in_y(to))
        def _():
            copy.start()

    for places in (fine_places, coarse_places):
        for place in EMPTY:
            places[place] = jnp.zeros((64, 64), BF16)
    for copy in copies[0]:
        copy.wait()
    build_weights(fine_places, fine_ahead, fine_behind, 0, len(GROUPS))

    for _, back, copy in y_copies:

        @pl.when(in_y(back))
        def _():
            copy.wait_recv()

    spread[...] = got[...].astype(F32)
    for row in range(2):
        own[pl.ds(row, 24, stride=8), :] = spread[0, pl.ds(row, 24, stride=2), :]
        own[pl.ds(6 + row, 24, stride=8), :] = spread[1, pl.ds(row, 24, stride=2), :]
    for q in range(2):
        for slots, zp, base in ((FINE_SLOTS, 4, 0), (COARSE_SLOTS, 2, 128)):
            for z in range(zp):
                start = base + (q * zp + z) * 16
                halo[1 + q, slots[1 + z]] = own[start : start + 16, :].astype(BF16)

    plane_copies = []
    for k, (sx, sz) in enumerate(PLANE):
        x_from, x_to, x_count = {-1: (1, 3, 1), 0: (1, 1, 2), 1: (2, 0, 1)}[sx]
        z_from, z_to, z_count = {-1: (2, 8, 2), 0: (2, 2, 6), 1: (6, 0, 2)}[sz]
        plane_copies.append((
            sx, sz, pltpu.make_async_remote_copy(
                src_ref=halo.at[pl.ds(x_from, x_count), pl.ds(z_from, z_count)],
                dst_ref=halo.at[pl.ds(x_to, x_count), pl.ds(z_to, z_count)],
                send_sem=plane_send.at[k], recv_sem=plane_recv.at[k],
                device_id=at_plane(sx, sz), device_id_type=MESH,
            )
        ))
    for sx, sz, copy in plane_copies:

        @pl.when(in_plane(sx, sz))
        def _():
            copy.start()

    for copy in copies[1]:
        copy.wait()
    build_weights(coarse_places, coarse_ahead, coarse_behind, 0, len(GROUPS))

    for sx, sz, copy in plane_copies:

        @pl.when(in_plane(-sx, -sz))
        def _():
            copy.wait_recv()

    shift_tiles(halo, odd, high, low)
    tiles[...] = level(halo, odd, high, low, fine_ahead, fine_behind, FINE_SLOTS)
    unpack_level(fine_out, tiles, 8)
    tiles[0:64, :] = level(halo, odd, high, low, coarse_ahead, coarse_behind, COARSE_SLOTS)
    unpack_level(coarse_out, tiles, 4)

    for to, _, copy in y_copies:

        @pl.when(in_y(to))
        def _():
            copy.wait_send()

    for sx, sz, copy in plane_copies:

        @pl.when(in_plane(sx, sz))
        def _():
            copy.wait_send()


def body(sizes, fine_multipoles, fine_translations, coarse_multipoles, coarse_translations):
    vmem = pl.BlockSpec(memory_space=pltpu.VMEM)
    hbm = pl.BlockSpec(memory_space=pl.ANY)
    groups = len(GROUPS)
    return pl.pallas_call(
        functools.partial(kernel, sizes),
        out_shape=[
            jax.ShapeDtypeStruct(fine_multipoles.shape, F32),
            jax.ShapeDtypeStruct(coarse_multipoles.shape, F32),
        ],
        in_specs=[vmem, hbm, vmem, hbm],
        out_specs=[vmem, vmem],
        scratch_shapes=[
            pltpu.VMEM((PLACES, 64, 64), BF16),
            pltpu.VMEM((PLACES, 64, 64), BF16),
            pltpu.VMEM((groups, 128, 384), BF16),
            pltpu.VMEM((groups, 384, 128), BF16),
            pltpu.VMEM((groups, 128, 384), BF16),
            pltpu.VMEM((groups, 384, 128), BF16),
            pltpu.VMEM((4, SLOTS, 16, 128), BF16),
            pltpu.VMEM((3, SLOTS, 16, 128), BF16),
            pltpu.VMEM((2, SLOTS, 16, 128), BF16),
            pltpu.VMEM((2, SLOTS, 16, 128), BF16),
            pltpu.VMEM((128, 128), F32),
            pltpu.VMEM((192, 128), F32),
            pltpu.VMEM((2, 48, 128), F32),
            pltpu.VMEM((2, 48, 128), BF16),
            pltpu.VMEM((2, 48, 128), BF16),
            pltpu.VMEM((2, 48, 128), F32),
            pltpu.VMEM((128, 128), F32),
            pltpu.SemaphoreType.DMA((2, len(RUNS))),
            pltpu.SemaphoreType.DMA((2,)),
            pltpu.SemaphoreType.DMA((2,)),
            pltpu.SemaphoreType.DMA((8,)),
            pltpu.SemaphoreType.DMA((8,)),
        ],
        compiler_params=pltpu.CompilerParams(
            collective_id=0, has_side_effects=True, vmem_limit_bytes=40 * 1024 * 1024
        ),
        name="translate",
    )(fine_multipoles, fine_translations, coarse_multipoles, coarse_translations)


def solution(mesh):
    sizes = tuple(mesh.shape[axis] for axis in ("gx", "gy", "gz"))
    return jax.shard_map(
        functools.partial(body, sizes),
        mesh=mesh,
        in_specs=(P("gx", "gy", "gz", None), P(), P("gx", "gy", "gz", None), P()),
        out_specs=(P("gx", "gy", "gz", None), P("gx", "gy", "gz", None)),
        check_vma=False,
    )
```

profile of v0, /device:TPU:1, one launch (start us, length us, event | category | flops | bytes accessed | tf_op | source)
XLA Modules:
  0.0 51.1 jit_solution(10620363068141182288)
XLA Ops:
  0.6 4.1 %copy.6.fine_table = bf16[158,64,64]{2,1,0:T(8,128)(2,1)S(1)} copy(bf16[158,64,64]{0,2,1:T(8,128)(2,1)} %param.5) | data formatting | bytes 2588672 | tf_op args[1]
  4.7 0.0 copy-start.1
  4.8 0.0 copy-start.2
  4.8 5.1 %copy.7.coarse_table = bf16[158,64,64]{2,1,0:T(8,128)(2,1)} copy(bf16[158,64,64]{0,2,1:T(8,128)(2,1)} %param.7) | data formatting | bytes 2588672 | tf_op args[3]
  9.8 0.0 copy-done.1
  9.9 0.0 copy-done.2
  9.9 0.0 copy-start
  9.9 1.7 %copy-done = bf16[158,64,64]{2,1,0:T(8,128)(2,1)S(1)} copy-done((bf16[158,64,64]{2,1,0:T(8,128)(2,1)S(1)}, bf16[158,64,64]{2,1,0:T(8,128)(2,1)}, u32[]{:S(2)}) %copy-start) | copy-done | bytes 1294360
  11.6 38.2 %translate.1 = (f32[4,4,8,64]{3,2,1,0:T(8,128)S(1)}, f32[4,4,4,64]{3,2,1,0:T(4,128)S(1)}) custom-call(bf16[4,4,8,64]{3,2,1,0:T(8,128)(2,1)S(1)} %copy-done.1, bf16[158,64,64]{2,1,0:T(8,128)(2,1)S(1)} %copy.6.fine_table, bf16[4,4,4,64]{3,2,1,0:T(4,128)(2,1)S(1)} %copy-done.2, bf16[158,64,64]{2,1,0:T(8,128)(2,1)S(1)} %copy-done), custom_call_target="tpu_custom_call" | custom-call | tf_op jit(solution)/shard_map/translate/pallas_call | solution.py:330
  49.8 0.6 %copy.10 = f32[4,4,8,64]{3,2,1,0:T(8,128)} copy(f32[4,4,8,64]{3,2,1,0:T(8,128)S(1)} %get-tuple-element.4) | data formatting | bytes 65536
  50.4 0.6 %copy.11 = f32[4,4,4,64]{3,2,1,0:T(4,128)} copy(f32[4,4,4,64]{3,2,1,0:T(4,128)S(1)} %get-tuple-element.5) | data formatting | bytes 32768
Async XLA Ops:
  4.7 5.1 %copy-start.1 = (bf16[4,4,8,64]{3,2,1,0:T(8,128)(2,1)S(1)}, bf16[4,4,8,64]{3,2,1,0:T(8,128)(2,1)}, u32[]{:S(2)}) copy-start(bf16[4,4,8,64]{3,2,1,0:T(8,128)(2,1)} %fine.1) | copy-start | bytes 49156
  4.8 5.1 %copy-start.2 = (bf16[4,4,4,64]{3,2,1,0:T(4,128)(2,1)S(1)}, bf16[4,4,4,64]{3,2,1,0:T(4,128)(2,1)}, u32[]{:S(2)}) copy-start(bf16[4,4,4,64]{3,2,1,0:T(4,128)(2,1)} %coarse.1) | copy-start | bytes 24580
  9.9 1.7 %copy-start = (bf16[158,64,64]{2,1,0:T(8,128)(2,1)S(1)}, bf16[158,64,64]{2,1,0:T(8,128)(2,1)}, u32[]{:S(2)}) copy-start(bf16[158,64,64]{2,1,0:T(8,128)(2,1)} %copy.7.coarse_table) | copy-start | bytes 3883012
where the time goes:
time: 51.4 us; the launch traced here: 51.1 us
  Pallas kernels  38.2 us (74%)
  local copies, waits for them, and re-layouts  12.2 us (24%)
  between operations  0.67 us (1%)
    pallas_call x1, Pallas kernels, body(): pl.pallas_call(functools.partial(kernel, sizes), out_shape=[jax.ShapeDtyp...  38.2 us
    unnamed x10, local copies, waits for them, and re-layouts  12.2 us

commit v1 on v0

--- a/solution.py
+++ b/solution.py
@@ -13,7 +13,7 @@
 F32 = jnp.float32
 
 GROUPS = [(0, ey) for ey in range(4)] + [(ex, ey) for ex in range(1, 4) for ey in range(-3, 4)]
-PLACES = 7 * len(GROUPS)
+OFFSETS = 158
 Y_PAIRS = ((-3, -2), (-1, 0), (1, 2), (3,))
 PLANE = [(sx, sz) for sx in (-1, 0, 1) for sz in (-1, 0, 1) if (sx, sz) != (0, 0)]
 FINE_SLOTS = (0, 2, 4, 5, 6, 8)
@@ -37,20 +37,11 @@
     return listed
 
 
-def table_runs():
-    places = [group(x, y) * 7 + z + 3 for x, y, z in half_offsets()]
-    runs = []
-    for index, place in enumerate(places):
-        cut = place in (4 * 7, 11 * 7, 18 * 7)
-        if runs and runs[-1][1] + runs[-1][2] == place and not cut:
-            runs[-1][2] += 1
-        else:
-            runs.append([index, place, 1])
-    empty = [place for place in range(PLACES) if place not in set(places)]
-    return [tuple(run) for run in runs], empty
-
-
-RUNS, EMPTY = table_runs()
+def place_selection():
+    picks = np.zeros((8 * len(GROUPS), OFFSETS), np.float32)
+    for index, (x, y, z) in enumerate(half_offsets()):
+        picks[8 * group(x, y) + z + 3, index] = 1.0
+    return picks
 
 
 def pack_level(src, stage, own, up, down, nz, base, msg_base):
@@ -78,15 +69,34 @@
             dst[x, y, pl.ds(1, zp, stride=2), :] = both[:, 64:128]
 
 
-def build_weights(places, ahead, behind, first, last):
+def turn_table(picks, table, turned, first, last):
+    @pl.loop(first, last)
+    def _(r):
+        rows = jnp.concatenate([table[r], table[32 + r]], axis=0)
+        classes = dot_ahead(picks[...], rows)
+        for g in range(len(GROUPS)):
+            turned[pl.ds(pl.multiple_of(g * 256 + r * 8, 8), 8), :] = classes[g * 8 : g * 8 + 8]
+
+
+def build_weights(turned, weights, first, last):
+    left = lax.broadcasted_iota(jnp.int32, (32, 128), 1) < 64
+
     @pl.loop(first, last)
     def _(g):
-        blocks = [places[g * 7 + e] for e in range(7)]
+        blocks = [turned[pl.ds(g * 256 + e, 32, stride=8), :] for e in range(7)]
+        swapped = [pltpu.roll(block, 64, 1) for block in blocks]
         for j in range(6):
-            pair = jnp.concatenate([blocks[j], blocks[j + 1]], axis=1)
-            half = 64 if j % 2 == 0 else 0
-            ahead[g, half : half + 64, (j // 2) * 128 : (j // 2) * 128 + 128] = pair
-            behind[g, (5 - j) * 64 : (5 - j) * 64 + 64, :] = pair
+            weights[g, j, 0:32] = jnp.where(left, blocks[j], swapped[j + 1]).astype(BF16)
+            weights[g, j, 32:64] = jnp.where(left, swapped[j], blocks[j + 1]).astype(BF16)
+
+
+def ahead(weights, g):
+    rows = [jnp.concatenate([weights[g, j + 2 * step] for step in range(3)], axis=1) for j in (1, 0)]
+    return jnp.concatenate(rows, axis=0)
+
+
+def behind(weights, g):
+    return jnp.concatenate([weights[g, 5 - s] for s in range(6)], axis=0)
 
 
 def shift_tiles(halo, odd, high, low):
@@ -128,7 +138,7 @@
     return lax.dot_general(left, weights, (((1,), (0,)), ((), ())), preferred_element_type=F32)
 
 
-def level(halo, odd, high, low, ahead, behind, slots):
+def level(halo, odd, high, low, weights, slots):
     get = functools.partial(sources, halo, odd, high, low, slots=slots)
     forward = {x: get(x) for x in range(0, 4)}
     backward = {x: get(-x) for x in range(0, 4)}
@@ -139,19 +149,19 @@
         xs = range(0, 4) if min(pair) >= 0 else range(1, 4)
         left = jnp.concatenate([forward[x] for x in xs], axis=1)
         right = jnp.concatenate(
-            [jnp.concatenate([ahead[group(x, ey)] for x in xs], axis=1) for ey in pair], axis=0
+            [jnp.concatenate([ahead(weights, group(x, ey)) for x in xs], axis=1) for ey in pair], axis=0
         )
         sums = dot_ahead(left, right)
         xs = range(0, 4) if max(pair) <= 0 else range(1, 4)
         left = jnp.concatenate([backward[x] for x in xs], axis=1)
         right = jnp.concatenate(
-            [jnp.concatenate([behind[group(x, -ey)] for x in xs], axis=0) for ey in pair], axis=1
+            [jnp.concatenate([behind(weights, group(x, -ey)) for x in xs], axis=0) for ey in pair], axis=1
         )
         sums = sums + dot_behind(left, right)
         for place, ey in enumerate(pair):
             term = sums[:, place * 128 : place * 128 + 128]
             if ey == 0:
-                term = term + dot_ahead(forward[0], ahead[group(0, 0)])
+                term = term + dot_ahead(forward[0], ahead(weights, group(0, 0)))
             term = term.reshape(rows // 8, 8, 128)
             term = pltpu.roll(term, (-(2 + ey)) % 8, 1)
             if ey == 3:
@@ -163,25 +173,23 @@
 
 
 def kernel(
-    sizes, fine, fine_table, coarse, coarse_table, fine_out, coarse_out,
-    fine_places, coarse_places, fine_ahead, fine_behind, coarse_ahead, coarse_behind,
+    sizes, picks, fine_hbm, fine_table_hbm, coarse_hbm, coarse_table_hbm, fine_out, coarse_out,
+    fine, coarse, fine_table, coarse_table, turned, fine_weights, coarse_weights,
     halo, odd, high, low, stage, own, faces, sent, got, spread, tiles,
-    table_sem, y_send, y_recv, plane_send, plane_recv,
+    load_sem, y_send, y_recv, plane_send, plane_recv,
 ):
     nx, ny, nz = sizes
     gx, gy, gz = lax.axis_index("gx"), lax.axis_index("gy"), lax.axis_index("gz")
 
-    copies = []
-    for at, (table, places) in enumerate(((fine_table, fine_places), (coarse_table, coarse_places))):
-        copies.append([
-            pltpu.make_async_copy(
-                table.at[pl.ds(c, n)], places.at[pl.ds(p, n)], table_sem.at[at, k]
-            )
-            for k, (c, p, n) in enumerate(RUNS)
-        ])
-    for some in copies:
-        for copy in some:
-            copy.start()
+    loads = [
+        pltpu.make_async_copy(src, dst, load_sem.at[k])
+        for k, (src, dst) in enumerate((
+            (fine_hbm, fine), (coarse_hbm, coarse),
+            (fine_table_hbm, fine_table), (coarse_table_hbm, coarse_table),
+        ))
+    ]
+    for load in loads:
+        load.start()
 
     @pl.when(gx == 0)
     def _():
@@ -235,6 +243,8 @@
         def _():
             pl.semaphore_signal(barrier, inc=1, device_id=at_plane(sx, sz), device_id_type=MESH)
 
+    loads[0].wait()
+    loads[1].wait()
     pack_level(fine, stage, own, faces.at[0], faces.at[1], 8, 0, 0)
     pack_level(coarse, stage, own, faces.at[0], faces.at[1], 4, 128, 32)
     sent[...] = faces[...].astype(BF16)
@@ -253,12 +263,9 @@
         def _():
             copy.start()
 
-    for places in (fine_places, coarse_places):
-        for place in EMPTY:
-            places[place] = jnp.zeros((64, 64), BF16)
-    for copy in copies[0]:
-        copy.wait()
-    build_weights(fine_places, fine_ahead, fine_behind, 0, len(GROUPS))
+    loads[2].wait()
+    turn_table(picks, fine_table, turned, 0, 32)
+    build_weights(turned, fine_weights, 0, len(GROUPS))
 
     for _, back, copy in y_copies:
 
@@ -294,9 +301,9 @@
         def _():
             copy.start()
 
-    for copy in copies[1]:
-        copy.wait()
-    build_weights(coarse_places, coarse_ahead, coarse_behind, 0, len(GROUPS))
+    loads[3].wait()
+    turn_table(picks, coarse_table, turned, 0, 32)
+    build_weights(turned, coarse_weights, 0, len(GROUPS))
 
     for sx, sz, copy in plane_copies:
 
@@ -305,9 +312,9 @@
             copy.wait_recv()
 
     shift_tiles(halo, odd, high, low)
-    tiles[...] = level(halo, odd, high, low, fine_ahead, fine_behind, FINE_SLOTS)
+    tiles[...] = level(halo, odd, high, low, fine_weights, FINE_SLOTS)
     unpack_level(fine_out, tiles, 8)
-    tiles[0:64, :] = level(halo, odd, high, low, coarse_ahead, coarse_behind, COARSE_SLOTS)
+    tiles[0:64, :] = level(halo, odd, high, low, coarse_weights, COARSE_SLOTS)
     unpack_level(coarse_out, tiles, 4)
 
     for to, _, copy in y_copies:
@@ -333,15 +340,16 @@
             jax.ShapeDtypeStruct(fine_multipoles.shape, F32),
             jax.ShapeDtypeStruct(coarse_multipoles.shape, F32),
         ],
-        in_specs=[vmem, hbm, vmem, hbm],
+        in_specs=[vmem, hbm, hbm, hbm, hbm],
         out_specs=[vmem, vmem],
         scratch_shapes=[
-            pltpu.VMEM((PLACES, 64, 64), BF16),
-            pltpu.VMEM((PLACES, 64, 64), BF16),
-            pltpu.VMEM((groups, 128, 384), BF16),
-            pltpu.VMEM((groups, 384, 128), BF16),
-            pltpu.VMEM((groups, 128, 384), BF16),
-            pltpu.VMEM((groups, 384, 128), BF16),
+            pltpu.VMEM(fine_multipoles.shape, BF16),
+            pltpu.VMEM(coarse_multipoles.shape, BF16),
+            pltpu.VMEM((64, 64, OFFSETS), BF16),
+            pltpu.VMEM((64, 64, OFFSETS), BF16),
+            pltpu.VMEM((groups * 256, 128), F32),
+            pltpu.VMEM((groups, 6, 64, 128), BF16),
+            pltpu.VMEM((groups, 6, 64, 128), BF16),
             pltpu.VMEM((4, SLOTS, 16, 128), BF16),
             pltpu.VMEM((3, SLOTS, 16, 128), BF16),
             pltpu.VMEM((2, SLOTS, 16, 128), BF16),
@@ -353,17 +361,23 @@
             pltpu.VMEM((2, 48, 128), BF16),
             pltpu.VMEM((2, 48, 128), F32),
             pltpu.VMEM((128, 128), F32),
-            pltpu.SemaphoreType.DMA((2, len(RUNS))),
+            pltpu.SemaphoreType.DMA((4,)),
             pltpu.SemaphoreType.DMA((2,)),
             pltpu.SemaphoreType.DMA((2,)),
             pltpu.SemaphoreType.DMA((8,)),
             pltpu.SemaphoreType.DMA((8,)),
         ],
         compiler_params=pltpu.CompilerParams(
-            collective_id=0, has_side_effects=True, vmem_limit_bytes=40 * 1024 * 1024
+            collective_id=0, has_side_effects=True, vmem_limit_bytes=56 * 1024 * 1024
         ),
         name="translate",
-    )(fine_multipoles, fine_translations, coarse_multipoles, coarse_translations)
+    )(
+        jnp.asarray(place_selection(), BF16),
+        fine_multipoles,
+        jnp.transpose(fine_translations, (1, 2, 0)),
+        coarse_multipoles,
+        jnp.transpose(coarse_translations, (1, 2, 0)),
+    )
 
 
 def solution(mesh):

time: 51.4 us -> 46.5 us (0.905)
  local copies, waits for them, and re-layouts: 12.2 us -> 2.85 us
  Pallas kernels: 38.2 us -> 42.2 us
    unnamed x10 -> x2, local copies, waits for them, and re-layouts: 12.2 us -> 2.85 us
    pallas_call x1, Pallas kernels: 38.2 us -> 42.2 us  [body(): pl.pallas_call(functools.partial(kernel, sizes), out_shape=[jax.ShapeDtyp...]
where the time goes in v1:
time: 46.5 us; the launch traced here: 45.7 us
  Pallas kernels  42.2 us (91%)
  local copies, waits for them, and re-layouts  2.85 us (6%)
  between operations  0.64 us (1%)
    pallas_call x1, Pallas kernels, body(): pl.pallas_call(functools.partial(kernel, sizes), out_shape=[jax.ShapeDtyp...  42.2 us
    unnamed x2, local copies, waits for them, and re-layouts  2.85 us

profile of v1, /device:TPU:1, one launch (start us, length us, event | category | flops | bytes accessed | tf_op | source)
XLA Modules:
  0.0 45.7 jit_solution(16131713114933725454)
XLA Ops:
  0.6 42.2 %translate.1 = (f32[4,4,8,64]{3,2,1,0:T(8,128)}, f32[4,4,4,64]{3,2,1,0:T(4,128)}) custom-call(bf16[200,158]{1,0:T(8,128)(2,1)} %constant.2.clone.picks, bf16[4,4,8,64]{3,2,1,0:T(8,128)(2,1)} %fine_hbm.1, bf16[64,64,158]{2,1,0:T(8,128)(2,1)} %bitcast.2, bf16[4,4,4,64]{3,2,1,0:T(4,128)(2,1)} %coarse_hbm.1, bf16[64,64,158]{2,1,0:T(8,128)(2,1)} %bitcast.3), custom_call_target="tpu_custom_call" | custom-call | tf_op jit(solution)/shard_map/translate/pallas_call | solution.py:337
  42.9 1.5 %copy.9 = f32[4,4,8,64]{3,2,1,0:T(8,128)} copy(f32[4,4,8,64]{3,2,1,0:T(8,128)} %get-tuple-element.4) | data formatting | bytes 65536
  44.3 1.4 %copy.10 = f32[4,4,4,64]{3,2,1,0:T(4,128)} copy(f32[4,4,4,64]{3,2,1,0:T(4,128)} %get-tuple-element.5) | data formatting | bytes 32768

commit v2 on v1

--- a/solution.py
+++ b/solution.py
@@ -19,6 +19,7 @@
 FINE_SLOTS = (0, 2, 4, 5, 6, 8)
 COARSE_SLOTS = (1, 3, 7, 9)
 SLOTS = 10
+TURN = 8
 
 
 def group(ex, ey):
@@ -69,25 +70,33 @@
             dst[x, y, pl.ds(1, zp, stride=2), :] = both[:, 64:128]
 
 
-def turn_table(picks, table, turned, first, last):
-    @pl.loop(first, last)
-    def _(r):
-        rows = jnp.concatenate([table[r], table[32 + r]], axis=0)
-        classes = dot_ahead(picks[...], rows)
-        for g in range(len(GROUPS)):
-            turned[pl.ds(pl.multiple_of(g * 256 + r * 8, 8), 8), :] = classes[g * 8 : g * 8 + 8]
-
-
-def build_weights(turned, weights, first, last):
+def turn_table(picks, table, turned):
+    @pl.loop(0, 32 // TURN)
+    def _(step):
+        for at in range(0, TURN, 2):
+            first = step * TURN + at
+            rows = jnp.concatenate(
+                [table[first], table[32 + first], table[first + 1], table[33 + first]], axis=0
+            )
+            classes = dot_ahead(picks[...], rows)
+            for g in range(len(GROUPS)):
+                start = pl.multiple_of(g * 256 + first * 8, 8)
+                turned[pl.ds(start, 8), :] = classes[g * 8 : g * 8 + 8, 0:128]
+                turned[pl.ds(start + 8, 8), :] = classes[g * 8 : g * 8 + 8, 128:256]
+
+
+def build_weights(turned, weights):
     left = lax.broadcasted_iota(jnp.int32, (32, 128), 1) < 64
 
-    @pl.loop(first, last)
-    def _(g):
-        blocks = [turned[pl.ds(g * 256 + e, 32, stride=8), :] for e in range(7)]
-        swapped = [pltpu.roll(block, 64, 1) for block in blocks]
-        for j in range(6):
-            weights[g, j, 0:32] = jnp.where(left, blocks[j], swapped[j + 1]).astype(BF16)
-            weights[g, j, 32:64] = jnp.where(left, swapped[j], blocks[j + 1]).astype(BF16)
+    @pl.loop(0, len(GROUPS) // 5)
+    def _(step):
+        for at in range(5):
+            g = step * 5 + at
+            blocks = [turned[pl.ds(g * 256 + e, 32, stride=8), :] for e in range(7)]
+            swapped = [pltpu.roll(block, 64, 1) for block in blocks]
+            for j in range(6):
+                weights[g, j, 0:32] = jnp.where(left, blocks[j], swapped[j + 1]).astype(BF16)
+                weights[g, j, 32:64] = jnp.where(left, swapped[j], blocks[j + 1]).astype(BF16)
 
 
 def ahead(weights, g):
@@ -173,10 +182,10 @@
 
 
 def kernel(
-    sizes, picks, fine_hbm, fine_table_hbm, coarse_hbm, coarse_table_hbm, fine_out, coarse_out,
-    fine, coarse, fine_table, coarse_table, turned, fine_weights, coarse_weights,
+    sizes, picks_hbm, fine_hbm, fine_table_hbm, coarse_hbm, coarse_table_hbm, fine_out, coarse_out,
+    picks, fine, coarse, fine_table, coarse_table, turned, fine_weights, coarse_weights,
     halo, odd, high, low, stage, own, faces, sent, got, spread, tiles,
-    load_sem, y_send, y_recv, plane_send, plane_recv,
+    load_sem, y_send, y_recv, plane_send, plane_recv, ready,
 ):
     nx, ny, nz = sizes
     gx, gy, gz = lax.axis_index("gx"), lax.axis_index("gy"), lax.axis_index("gz")
@@ -184,37 +193,13 @@
     loads = [
         pltpu.make_async_copy(src, dst, load_sem.at[k])
         for k, (src, dst) in enumerate((
-            (fine_hbm, fine), (coarse_hbm, coarse),
+            (fine_hbm, fine), (coarse_hbm, coarse), (picks_hbm, picks),
             (fine_table_hbm, fine_table), (coarse_table_hbm, coarse_table),
         ))
     ]
     for load in loads:
         load.start()
 
-    @pl.when(gx == 0)
-    def _():
-        halo[0] = jnp.zeros((SLOTS, 16, 128), BF16)
-
-    @pl.when(gx == nx - 1)
-    def _():
-        halo[3] = jnp.zeros((SLOTS, 16, 128), BF16)
-
-    @pl.when(gz == 0)
-    def _():
-        halo[:, 0:2] = jnp.zeros((4, 2, 16, 128), BF16)
-
-    @pl.when(gz == nz - 1)
-    def _():
-        halo[:, 8:10] = jnp.zeros((4, 2, 16, 128), BF16)
-
-    @pl.when(gy == 0)
-    def _():
-        got[0] = jnp.zeros((48, 128), BF16)
-
-    @pl.when(gy == ny - 1)
-    def _():
-        got[1] = jnp.zeros((48, 128), BF16)
-
     def in_y(sy):
         return (gy + sy >= 0) & (gy + sy < ny)
 
@@ -227,17 +212,19 @@
     def at_plane(sx, sz):
         return (lax.rem(gx + sx + nx, nx), gy, lax.rem(gz + sz + nz, nz))
 
+    phase = lax.rem(gy, 4)
+    waits = {1: phase >= 2, -1: (phase == 1) | (phase == 2)}
     barrier = pltpu.get_barrier_semaphore()
-    neighbours = jnp.int32(0)
+    greetings = jnp.int32(0)
     for sy in (1, -1):
-        neighbours += in_y(sy).astype(jnp.int32)
-
-        @pl.when(in_y(sy))
+        greetings += (in_y(sy) & waits[sy]).astype(jnp.int32)
+
+        @pl.when(in_y(sy) & jnp.logical_not(waits[sy]))
         def _():
             pl.semaphore_signal(barrier, inc=1, device_id=at_y(sy), device_id_type=MESH)
 
     for sx, sz in PLANE:
-        neighbours += in_plane(sx, sz).astype(jnp.int32)
+        greetings += in_plane(sx, sz).astype(jnp.int32)
 
         @pl.when(in_plane(sx, sz))
         def _():
@@ -250,26 +237,62 @@
     sent[...] = faces[...].astype(BF16)
 
     y_copies = [
-        (sy, -sy, pltpu.make_async_remote_copy(
+        (sy, pltpu.make_async_remote_copy(
             src_ref=sent.at[k], dst_ref=got.at[k], send_sem=y_send.at[k], recv_sem=y_recv.at[k],
             device_id=at_y(sy), device_id_type=MESH,
         ))
         for k, sy in enumerate((1, -1))
     ]
-    pl.semaphore_wait(barrier, neighbours)
-    for to, _, copy in y_copies:
-
-        @pl.when(in_y(to))
+    pl.semaphore_wait(barrier, greetings)
+    for k, (sy, copy) in enumerate(y_copies):
+
+        @pl.when(in_y(sy) & waits[sy])
         def _():
             copy.start()
+            pl.semaphore_signal(ready.at[1 - k], inc=1, device_id=at_y(sy), device_id_type=MESH)
+
+    @pl.when(gx == 0)
+    def _():
+        halo[0] = jnp.zeros((SLOTS, 16, 128), BF16)
+
+    @pl.when(gx == nx - 1)
+    def _():
+        halo[3] = jnp.zeros((SLOTS, 16, 128), BF16)
+
+    @pl.when(gz == 0)
+    def _():
+        halo[:, 0:2] = jnp.zeros((4, 2, 16, 128), BF16)
+
+    @pl.when(gz == nz - 1)
+    def _():
+        halo[:, 8:10] = jnp.zeros((4, 2, 16, 128), BF16)
+
+    @pl.when(gy == 0)
+    def _():
+        got[0] = jnp.zeros((48, 128), BF16)
+
+    @pl.when(gy == ny - 1)
+    def _():
+        got[1] = jnp.zeros((48, 128), BF16)
 
     loads[2].wait()
-    turn_table(picks, fine_table, turned, 0, 32)
-    build_weights(turned, fine_weights, 0, len(GROUPS))
-
-    for _, back, copy in y_copies:
-
-        @pl.when(in_y(back))
+    loads[3].wait()
+    turn_table(picks, fine_table, turned)
+    build_weights(turned, fine_weights)
+    loads[4].wait()
+    turn_table(picks, coarse_table, turned)
+    build_weights(turned, coarse_weights)
+
+    for k, (sy, copy) in enumerate(y_copies):
+
+        @pl.when(in_y(sy) & jnp.logical_not(waits[sy]))
+        def _():
+            pl.semaphore_wait(ready.at[k], 1)
+            copy.start()
+
+    for sy, copy in y_copies:
+
+        @pl.when(in_y(-sy))
         def _():
             copy.wait_recv()
 
@@ -301,10 +324,6 @@
         def _():
             copy.start()
 
-    loads[3].wait()
-    turn_table(picks, coarse_table, turned, 0, 32)
-    build_weights(turned, coarse_weights, 0, len(GROUPS))
-
     for sx, sz, copy in plane_copies:
 
         @pl.when(in_plane(-sx, -sz))
@@ -317,9 +336,9 @@
     tiles[0:64, :] = level(halo, odd, high, low, coarse_weights, COARSE_SLOTS)
     unpack_level(coarse_out, tiles, 4)
 
-    for to, _, copy in y_copies:
-
-        @pl.when(in_y(to))
+    for sy, copy in y_copies:
+
+        @pl.when(in_y(sy))
         def _():
             copy.wait_send()
 
@@ -337,12 +356,13 @@
     return pl.pallas_call(
         functools.partial(kernel, sizes),
         out_shape=[
-            jax.ShapeDtypeStruct(fine_multipoles.shape, F32),
-            jax.ShapeDtypeStruct(coarse_multipoles.shape, F32),
+            pltpu.VMEM(fine_multipoles.shape, F32),
+            pltpu.VMEM(coarse_multipoles.shape, F32),
         ],
-        in_specs=[vmem, hbm, hbm, hbm, hbm],
+        in_specs=[hbm] * 5,
         out_specs=[vmem, vmem],
         scratch_shapes=[
+            pltpu.VMEM((8 * groups, OFFSETS), BF16),
             pltpu.VMEM(fine_multipoles.shape, BF16),
             pltpu.VMEM(coarse_multipoles.shape, BF16),
             pltpu.VMEM((64, 64, OFFSETS), BF16),
@@ -361,23 +381,27 @@
             pltpu.VMEM((2, 48, 128), BF16),
             pltpu.VMEM((2, 48, 128), F32),
             pltpu.VMEM((128, 128), F32),
-            pltpu.SemaphoreType.DMA((4,)),
+            pltpu.SemaphoreType.DMA((5,)),
             pltpu.SemaphoreType.DMA((2,)),
             pltpu.SemaphoreType.DMA((2,)),
             pltpu.SemaphoreType.DMA((8,)),
             pltpu.SemaphoreType.DMA((8,)),
+            pltpu.SemaphoreType.REGULAR((2,)),
         ],
         compiler_params=pltpu.CompilerParams(
-            collective_id=0, has_side_effects=True, vmem_limit_bytes=56 * 1024 * 1024
+            collective_id=0, has_side_effects=True, vmem_limit_bytes=24 * 1024 * 1024
         ),
         name="translate",
-    )(
-        jnp.asarray(place_selection(), BF16),
-        fine_multipoles,
-        jnp.transpose(fine_translations, (1, 2, 0)),
-        coarse_multipoles,
-        jnp.transpose(coarse_translations, (1, 2, 0)),
-    )
+    )(*(
+        pltpu.with_memory_space_constraint(array, pltpu.HBM)
+        for array in (
+            jnp.asarray(place_selection(), BF16),
+            fine_multipoles,
+            jnp.transpose(fine_translations, (1, 2, 0)),
+            coarse_multipoles,
+            jnp.transpose(coarse_translations, (1, 2, 0)),
+        )
+    ))
 
 
 def solution(mesh):

time: 46.5 us -> 33.8 us (0.73)
  the two profiles are of different devices: /device:TPU:1 before, /device:TPU:29 now
where the time goes in v2:
time: 33.8 us; the launch traced here: 33.6 us
  Pallas kernels  31.7 us (94%)
  local copies, waits for them, and re-layouts  1.25 us (4%)
  between operations  0.64 us (2%)
    pallas_call x1, Pallas kernels, body(): pl.pallas_call(functools.partial(kernel, sizes), out_shape=[pltpu.VMEM(fi...  31.7 us
    unnamed x2, local copies, waits for them, and re-layouts  1.25 us

profile of v2, /device:TPU:29, one launch (start us, length us, event | category | flops | bytes accessed | tf_op | source)
XLA Modules:
  0.0 33.6 jit_solution(3663814719682991138)
XLA Ops:
  0.6 31.7 %translate.1 = (f32[4,4,8,64]{3,2,1,0:T(8,128)S(1)}, f32[4,4,4,64]{3,2,1,0:T(4,128)S(1)}) custom-call(bf16[200,158]{1,0:T(8,128)(2,1)} %constant.2.clone.picks_hbm, bf16[4,4,8,64]{3,2,1,0:T(8,128)(2,1)} %fine_hbm.1, bf16[64,64,158]{2,1,0:T(8,128)(2,1)} %bitcast.2, bf16[4,4,4,64]{3,2,1,0:T(4,128)(2,1)} %coarse_hbm.1, bf16[64,64,158]{2,1,0:T(8,128)(2,1)} %bitcast.3), custom_call_target="tpu_custom_call" | custom-call | tf_op jit(solution)/shard_map/translate/pallas_call | solution.py:356
  32.4 0.6 %copy.9 = f32[4,4,8,64]{3,2,1,0:T(8,128)} copy(f32[4,4,8,64]{3,2,1,0:T(8,128)S(1)} %get-tuple-element.2) | data formatting | bytes 65536
  33.0 0.6 %copy.10 = f32[4,4,4,64]{3,2,1,0:T(4,128)} copy(f32[4,4,4,64]{3,2,1,0:T(4,128)S(1)} %get-tuple-element.3) | data formatting | bytes 32768

commit v3 on v2

--- a/solution.py
+++ b/solution.py
@@ -15,7 +15,7 @@
 GROUPS = [(0, ey) for ey in range(4)] + [(ex, ey) for ex in range(1, 4) for ey in range(-3, 4)]
 OFFSETS = 158
 Y_PAIRS = ((-3, -2), (-1, 0), (1, 2), (3,))
-PLANE = [(sx, sz) for sx in (-1, 0, 1) for sz in (-1, 0, 1) if (sx, sz) != (0, 0)]
+PLANE = [(-1, -1), (-1, 1), (1, -1), (1, 1), (0, -1), (0, 1), (-1, 0), (1, 0)]
 FINE_SLOTS = (0, 2, 4, 5, 6, 8)
 COARSE_SLOTS = (1, 3, 7, 9)
 SLOTS = 10
@@ -60,11 +60,11 @@
             face[pl.ds(msg_base + tile * 2 + y % 2, zp, stride=4), :] = both
 
 
-def unpack_level(dst, tiles, nz):
+def unpack_level(dst, tiles, nz, base):
     zp = nz // 2
     for x in range(4):
         for y in range(4):
-            start = ((x // 2) * zp * 2 + x % 2) * 8 + y
+            start = base + ((x // 2) * zp * 2 + x % 2) * 8 + y
             both = tiles[pl.ds(start, zp, stride=16), :]
             dst[x, y, pl.ds(0, zp, stride=2), :] = both[:, 0:64]
             dst[x, y, pl.ds(1, zp, stride=2), :] = both[:, 64:128]
@@ -182,9 +182,9 @@
 
 
 def kernel(
-    sizes, picks_hbm, fine_hbm, fine_table_hbm, coarse_hbm, coarse_table_hbm, fine_out, coarse_out,
+    sizes, picks_hbm, fine_hbm, fine_table_hbm, coarse_hbm, coarse_table_hbm, tiles,
     picks, fine, coarse, fine_table, coarse_table, turned, fine_weights, coarse_weights,
-    halo, odd, high, low, stage, own, faces, sent, got, spread, tiles,
+    halo, odd, high, low, stage, own, faces, sent, got, spread,
     load_sem, y_send, y_recv, plane_send, plane_recv, ready,
 ):
     nx, ny, nz = sizes
@@ -331,10 +331,8 @@
             copy.wait_recv()
 
     shift_tiles(halo, odd, high, low)
-    tiles[...] = level(halo, odd, high, low, fine_weights, FINE_SLOTS)
-    unpack_level(fine_out, tiles, 8)
-    tiles[0:64, :] = level(halo, odd, high, low, coarse_weights, COARSE_SLOTS)
-    unpack_level(coarse_out, tiles, 4)
+    tiles[0:128, :] = level(halo, odd, high, low, fine_weights, FINE_SLOTS)
+    tiles[128:192, :] = level(halo, odd, high, low, coarse_weights, COARSE_SLOTS)
 
     for sy, copy in y_copies:
 
@@ -347,20 +345,22 @@
         @pl.when(in_plane(sx, sz))
         def _():
             copy.wait_send()
+
+
+def place(tiles, fine_out, coarse_out):
+    unpack_level(fine_out, tiles, 8, 0)
+    unpack_level(coarse_out, tiles, 4, 128)
 
 
 def body(sizes, fine_multipoles, fine_translations, coarse_multipoles, coarse_translations):
     vmem = pl.BlockSpec(memory_space=pltpu.VMEM)
     hbm = pl.BlockSpec(memory_space=pl.ANY)
     groups = len(GROUPS)
-    return pl.pallas_call(
+    tiles = pl.pallas_call(
         functools.partial(kernel, sizes),
-        out_shape=[
-            pltpu.VMEM(fine_multipoles.shape, F32),
-            pltpu.VMEM(coarse_multipoles.shape, F32),
-        ],
+        out_shape=pltpu.VMEM((192, 128), F32),
         in_specs=[hbm] * 5,
-        out_specs=[vmem, vmem],
+        out_specs=vmem,
         scratch_shapes=[
             pltpu.VMEM((8 * groups, OFFSETS), BF16),
             pltpu.VMEM(fine_multipoles.shape, BF16),
@@ -380,7 +380,6 @@
             pltpu.VMEM((2, 48, 128), BF16),
             pltpu.VMEM((2, 48, 128), BF16),
             pltpu.VMEM((2, 48, 128), F32),
-            pltpu.VMEM((128, 128), F32),
             pltpu.SemaphoreType.DMA((5,)),
             pltpu.SemaphoreType.DMA((2,)),
             pltpu.SemaphoreType.DMA((2,)),
@@ -402,6 +401,16 @@
             jnp.transpose(coarse_translations, (1, 2, 0)),
         )
     ))
+    return pl.pallas_call(
+        place,
+        out_shape=[
+            jax.ShapeDtypeStruct(fine_multipoles.shape, F32),
+            jax.ShapeDtypeStruct(coarse_multipoles.shape, F32),
+        ],
+        in_specs=[vmem],
+        out_specs=[vmem, vmem],
+        name="place",
+    )(pltpu.with_memory_space_constraint(tiles, pltpu.VMEM))
 
 
 def solution(mesh):

time: 33.8 us -> 33.1 us (0.979)
  the two profiles are of different devices: /device:TPU:29 before, /device:TPU:27 now
where the time goes in v3:
time: 33.1 us; the launch traced here: 33 us
  Pallas kernels  32.4 us (98%)
  between operations  0.64 us (2%)
    pallas_call x1, Pallas kernels, body(): pl.pallas_call(functools.partial(kernel, sizes), out_shape=pltpu.VMEM((19...  31.6 us
    pallas_call x1, Pallas kernels, body(): pl.pallas_call(place, out_shape=[jax.ShapeDtypeStruct(fine_multipoles.sha...  0.72 us

profile of v3, /device:TPU:27, one launch (start us, length us, event | category | flops | bytes accessed | tf_op | source)
XLA Modules:
  0.0 33.0 jit_solution(13806169842839774562)
XLA Ops:
  0.6 31.6 %translate.1.tiles = f32[192,128]{1,0:T(8,128)S(1)} custom-call(bf16[200,158]{1,0:T(8,128)(2,1)} %constant.2.clone.picks_hbm, bf16[4,4,8,64]{3,2,1,0:T(8,128)(2,1)} %fine_hbm.1, bf16[64,64,158]{2,1,0:T(8,128)(2,1)} %bitcast.2, bf16[4,4,4,64]{3,2,1,0:T(4,128)(2,1)} %coarse_hbm.1, bf16[64,64,158]{2,1,0:T(8,128)(2,1)} %bitcast.3), custom_call_target="tpu_custom_call" | custom-call | tf_op jit(solution)/shard_map/translate/pallas_call | solution.py:359
  32.3 0.7 %place.1 = (f32[4,4,8,64]{3,2,1,0:T(8,128)}, f32[4,4,4,64]{3,2,1,0:T(4,128)}) custom-call(f32[192,128]{1,0:T(8,128)S(1)} %translate.1.tiles), custom_call_target="tpu_custom_call" | custom-call | tf_op jit(solution)/shard_map/place/pallas_call | solution.py:404

commit v4 on v3

--- a/solution.py
+++ b/solution.py
@@ -14,7 +14,8 @@
 
 GROUPS = [(0, ey) for ey in range(4)] + [(ex, ey) for ex in range(1, 4) for ey in range(-3, 4)]
 OFFSETS = 158
-Y_PAIRS = ((-3, -2), (-1, 0), (1, 2), (3,))
+OWN, BELOW, ABOVE = range(3)
+Y_PAIRS = (((-3, -2), (-1, 0), (1, 2), (3,)), ((-3, -2), (-1,)), ((1, 2), (3,)))
 PLANE = [(-1, -1), (-1, 1), (1, -1), (1, 1), (0, -1), (0, 1), (-1, 0), (1, 0)]
 FINE_SLOTS = (0, 2, 4, 5, 6, 8)
 COARSE_SLOTS = (1, 3, 7, 9)
@@ -147,14 +148,14 @@
     return lax.dot_general(left, weights, (((1,), (0,)), ((), ())), preferred_element_type=F32)
 
 
-def level(halo, odd, high, low, weights, slots):
+def level(halo, odd, high, low, weights, slots, slab):
     get = functools.partial(sources, halo, odd, high, low, slots=slots)
     forward = {x: get(x) for x in range(0, 4)}
     backward = {x: get(-x) for x in range(0, 4)}
     rows = forward[0].shape[0]
     y = lax.broadcasted_iota(jnp.int32, (rows // 8, 8, 128), 1)
     total = None
-    for pair in Y_PAIRS:
+    for pair in Y_PAIRS[slab]:
         xs = range(0, 4) if min(pair) >= 0 else range(1, 4)
         left = jnp.concatenate([forward[x] for x in xs], axis=1)
         right = jnp.concatenate(
@@ -232,8 +233,9 @@
 
     loads[0].wait()
     loads[1].wait()
-    pack_level(fine, stage, own, faces.at[0], faces.at[1], 8, 0, 0)
-    pack_level(coarse, stage, own, faces.at[0], faces.at[1], 4, 128, 32)
+    own[...] = jnp.zeros((3, 192, 128), F32)
+    pack_level(fine, stage, own.at[OWN], faces.at[0], faces.at[1], 8, 0, 0)
+    pack_level(coarse, stage, own.at[OWN], faces.at[0], faces.at[1], 4, 128, 32)
     sent[...] = faces[...].astype(BF16)
 
     y_copies = [
@@ -251,21 +253,90 @@
             copy.start()
             pl.semaphore_signal(ready.at[1 - k], inc=1, device_id=at_y(sy), device_id_type=MESH)
 
+    def plane_copies(slab):
+        made = []
+        for k, (sx, sz) in enumerate(PLANE):
+            x_from, x_to, x_count = {-1: (1, 3, 1), 0: (1, 1, 2), 1: (2, 0, 1)}[sx]
+            z_from, z_to, z_count = {-1: (2, 8, 2), 0: (2, 2, 6), 1: (6, 0, 2)}[sz]
+            made.append((
+                sx, sz, pltpu.make_async_remote_copy(
+                    src_ref=halo.at[slab, pl.ds(x_from, x_count), pl.ds(z_from, z_count)],
+                    dst_ref=halo.at[slab, pl.ds(x_to, x_count), pl.ds(z_to, z_count)],
+                    send_sem=plane_send.at[slab, k], recv_sem=plane_recv.at[slab, k],
+                    device_id=at_plane(sx, sz), device_id_type=MESH,
+                )
+            ))
+        return made
+
+    def share(slab):
+        for q in range(2):
+            for slots, zp, base in ((FINE_SLOTS, 4, 0), (COARSE_SLOTS, 2, 128)):
+                for z in range(zp):
+                    start = base + (q * zp + z) * 16
+                    halo[slab, 1 + q, slots[1 + z]] = own[slab, start : start + 16, :].astype(BF16)
+        copies = plane_copies(slab)
+        for sx, sz, copy in copies:
+
+            @pl.when(in_plane(sx, sz))
+            def _():
+                copy.start()
+
+        return copies
+
+    def use(slab, copies):
+        for sx, sz, copy in copies:
+
+            @pl.when(in_plane(-sx, -sz))
+            def _():
+                copy.wait_recv()
+
+        shift_tiles(halo.at[slab], odd, high, low)
+        for weights, slots, first, last in (
+            (fine_weights, FINE_SLOTS, 0, 128), (coarse_weights, COARSE_SLOTS, 128, 192),
+        ):
+            given = level(halo.at[slab], odd, high, low, weights, slots, slab)
+            if slab == OWN:
+                tiles[first:last, :] = given
+            else:
+                tiles[first:last, :] += given
+
+    def answer(k, when):
+        sy, copy = y_copies[k]
+
+        @pl.when(in_y(sy) & jnp.logical_not(waits[sy]) & when)
+        def _():
+            pl.semaphore_wait(ready.at[k], 1)
+            copy.start()
+
+    def receive(k, slab):
+        sy, copy = y_copies[k]
+
+        @pl.when(in_y(-sy))
+        def _():
+            copy.wait_recv()
+
+        spread[k] = got[k].astype(F32)
+        for row in range(2):
+            at = row if slab == BELOW else 6 + row
+            own[slab, pl.ds(at, 24, stride=8), :] = spread[k, pl.ds(row, 24, stride=2), :]
+
+    own_copies = share(OWN)
+
     @pl.when(gx == 0)
     def _():
-        halo[0] = jnp.zeros((SLOTS, 16, 128), BF16)
+        halo[:, 0] = jnp.zeros((3, SLOTS, 16, 128), BF16)
 
     @pl.when(gx == nx - 1)
     def _():
-        halo[3] = jnp.zeros((SLOTS, 16, 128), BF16)
+        halo[:, 3] = jnp.zeros((3, SLOTS, 16, 128), BF16)
 
     @pl.when(gz == 0)
     def _():
-        halo[:, 0:2] = jnp.zeros((4, 2, 16, 128), BF16)
+        halo[:, :, 0:2] = jnp.zeros((3, 4, 2, 16, 128), BF16)
 
     @pl.when(gz == nz - 1)
     def _():
-        halo[:, 8:10] = jnp.zeros((4, 2, 16, 128), BF16)
+        halo[:, :, 8:10] = jnp.zeros((3, 4, 2, 16, 128), BF16)
 
     @pl.when(gy == 0)
     def _():
@@ -283,64 +354,24 @@
     turn_table(picks, coarse_table, turned)
     build_weights(turned, coarse_weights)
 
-    for k, (sy, copy) in enumerate(y_copies):
-
-        @pl.when(in_y(sy) & jnp.logical_not(waits[sy]))
-        def _():
-            pl.semaphore_wait(ready.at[k], 1)
-            copy.start()
+    use(OWN, own_copies)
+    answer(0, phase < 2)
+    answer(1, phase == 3)
+    receive(1, ABOVE)
+    above_copies = share(ABOVE)
+    use(ABOVE, above_copies)
+    answer(1, phase == 0)
+    receive(0, BELOW)
+    below_copies = share(BELOW)
+    use(BELOW, below_copies)
 
     for sy, copy in y_copies:
 
-        @pl.when(in_y(-sy))
-        def _():
-            copy.wait_recv()
-
-    spread[...] = got[...].astype(F32)
-    for row in range(2):
-        own[pl.ds(row, 24, stride=8), :] = spread[0, pl.ds(row, 24, stride=2), :]
-        own[pl.ds(6 + row, 24, stride=8), :] = spread[1, pl.ds(row, 24, stride=2), :]
-    for q in range(2):
-        for slots, zp, base in ((FINE_SLOTS, 4, 0), (COARSE_SLOTS, 2, 128)):
-            for z in range(zp):
-                start = base + (q * zp + z) * 16
-                halo[1 + q, slots[1 + z]] = own[start : start + 16, :].astype(BF16)
-
-    plane_copies = []
-    for k, (sx, sz) in enumerate(PLANE):
-        x_from, x_to, x_count = {-1: (1, 3, 1), 0: (1, 1, 2), 1: (2, 0, 1)}[sx]
-        z_from, z_to, z_count = {-1: (2, 8, 2), 0: (2, 2, 6), 1: (6, 0, 2)}[sz]
-        plane_copies.append((
-            sx, sz, pltpu.make_async_remote_copy(
-                src_ref=halo.at[pl.ds(x_from, x_count), pl.ds(z_from, z_count)],
-                dst_ref=halo.at[pl.ds(x_to, x_count), pl.ds(z_to, z_count)],
-                send_sem=plane_send.at[k], recv_sem=plane_recv.at[k],
-                device_id=at_plane(sx, sz), device_id_type=MESH,
-            )
-        ))
-    for sx, sz, copy in plane_copies:
-
-        @pl.when(in_plane(sx, sz))
-        def _():
-            copy.start()
-
-    for sx, sz, copy in plane_copies:
-
-        @pl.when(in_plane(-sx, -sz))
-        def _():
-            copy.wait_recv()
-
-    shift_tiles(halo, odd, high, low)
-    tiles[0:128, :] = level(halo, odd, high, low, fine_weights, FINE_SLOTS)
-    tiles[128:192, :] = level(halo, odd, high, low, coarse_weights, COARSE_SLOTS)
-
-    for sy, copy in y_copies:
-
         @pl.when(in_y(sy))
         def _():
             copy.wait_send()
 
-    for sx, sz, copy in plane_copies:
+    for sx, sz, copy in own_copies + above_copies + below_copies:
 
         @pl.when(in_plane(sx, sz))
         def _():
@@ -370,12 +401,12 @@
             pltpu.VMEM((groups * 256, 128), F32),
             pltpu.VMEM((groups, 6, 64, 128), BF16),
             pltpu.VMEM((groups, 6, 64, 128), BF16),
-            pltpu.VMEM((4, SLOTS, 16, 128), BF16),
+            pltpu.VMEM((3, 4, SLOTS, 16, 128), BF16),
             pltpu.VMEM((3, SLOTS, 16, 128), BF16),
             pltpu.VMEM((2, SLOTS, 16, 128), BF16),
             pltpu.VMEM((2, SLOTS, 16, 128), BF16),
             pltpu.VMEM((128, 128), F32),
-            pltpu.VMEM((192, 128), F32),
+            pltpu.VMEM((3, 192, 128), F32),
             pltpu.VMEM((2, 48, 128), F32),
             pltpu.VMEM((2, 48, 128), BF16),
             pltpu.VMEM((2, 48, 128), BF16),
@@ -383,8 +414,8 @@
             pltpu.SemaphoreType.DMA((5,)),
             pltpu.SemaphoreType.DMA((2,)),
             pltpu.SemaphoreType.DMA((2,)),
-            pltpu.SemaphoreType.DMA((8,)),
-            pltpu.SemaphoreType.DMA((8,)),
+            pltpu.SemaphoreType.DMA((3, 8)),
+            pltpu.SemaphoreType.DMA((3, 8)),
             pltpu.SemaphoreType.REGULAR((2,)),
         ],
         compiler_params=pltpu.CompilerParams(

time: 33.1 us -> 36.9 us (1.11)
  the two profiles are of different devices: /device:TPU:27 before, /device:TPU:1 now
where the time goes in v4:
time: 36.9 us; the launch traced here: 36.7 us
  Pallas kernels  36.1 us (98%)
  between operations  0.64 us (2%)
    pallas_call x1, Pallas kernels, body(): pl.pallas_call(functools.partial(kernel, sizes), out_shape=pltpu.VMEM((19...  35.3 us

profile of v4, /device:TPU:1, one launch (start us, length us, event | category | flops | bytes accessed | tf_op | source)
XLA Modules:
  0.0 36.7 jit_solution(16228704806296712327)
XLA Ops:
  0.6 35.3 %translate.1.tiles = f32[192,128]{1,0:T(8,128)S(1)} custom-call(bf16[200,158]{1,0:T(8,128)(2,1)} %constant.2.clone.picks_hbm, bf16[4,4,8,64]{3,2,1,0:T(8,128)(2,1)} %fine_hbm.1, bf16[64,64,158]{2,1,0:T(8,128)(2,1)} %bitcast.2, bf16[4,4,4,64]{3,2,1,0:T(4,128)(2,1)} %coarse_hbm.1, bf16[64,64,158]{2,1,0:T(8,128)(2,1)} %bitcast.3), custom_call_target="tpu_custom_call" | custom-call | tf_op jit(solution)/shard_map/translate/pallas_call | solution.py:390
  36.0 0.7 %place.1 = (f32[4,4,8,64]{3,2,1,0:T(8,128)}, f32[4,4,4,64]{3,2,1,0:T(4,128)}) custom-call(f32[192,128]{1,0:T(8,128)S(1)} %translate.1.tiles), custom_call_target="tpu_custom_call" | custom-call | tf_op jit(solution)/shard_map/place/pallas_call | solution.py:435

commit v5 on v4

--- a/solution.py
+++ b/solution.py
@@ -299,6 +299,11 @@
                 tiles[first:last, :] = given
             else:
                 tiles[first:last, :] += given
+        for sx, sz, copy in copies:
+
+            @pl.when(in_plane(sx, sz))
+            def _():
+                copy.wait_send()
 
     def answer(k, when):
         sy, copy = y_copies[k]
@@ -337,14 +342,6 @@
     @pl.when(gz == nz - 1)
     def _():
         halo[:, :, 8:10] = jnp.zeros((3, 4, 2, 16, 128), BF16)
-
-    @pl.when(gy == 0)
-    def _():
-        got[0] = jnp.zeros((48, 128), BF16)
-
-    @pl.when(gy == ny - 1)
-    def _():
-        got[1] = jnp.zeros((48, 128), BF16)
 
     loads[2].wait()
     loads[3].wait()
@@ -357,23 +354,25 @@
     use(OWN, own_copies)
     answer(0, phase < 2)
     answer(1, phase == 3)
-    receive(1, ABOVE)
-    above_copies = share(ABOVE)
-    use(ABOVE, above_copies)
-    answer(1, phase == 0)
-    receive(0, BELOW)
-    below_copies = share(BELOW)
-    use(BELOW, below_copies)
+
+    @pl.loop(0, 2)
+    def _(step):
+        above = (step == 0) == (phase == 0)
+
+        @pl.when(above & in_y(1))
+        def _():
+            receive(1, ABOVE)
+            use(ABOVE, share(ABOVE))
+
+        @pl.when(jnp.logical_not(above) & in_y(-1))
+        def _():
+            answer(1, phase == 0)
+            receive(0, BELOW)
+            use(BELOW, share(BELOW))
 
     for sy, copy in y_copies:
 
         @pl.when(in_y(sy))
-        def _():
-            copy.wait_send()
-
-    for sx, sz, copy in own_copies + above_copies + below_copies:
-
-        @pl.when(in_plane(sx, sz))
         def _():
             copy.wait_send()
 

time: 36.9 us -> 32.9 us (0.89)
  the two profiles are of different devices: /device:TPU:1 before, /device:TPU:256 now
where the time goes in v5:
time: 32.9 us; the launch traced here: 32.7 us
  Pallas kernels  32.1 us (98%)
  between operations  0.64 us (2%)
    pallas_call x1, Pallas kernels, body(): pl.pallas_call(functools.partial(kernel, sizes), out_shape=pltpu.VMEM((19...  31.4 us
    pallas_call x1, Pallas kernels, body(): pl.pallas_call(place, out_shape=[jax.ShapeDtypeStruct(fine_multipoles.sha...  0.72 us

profile of v5, /device:TPU:256, one launch (start us, length us, event | category | flops | bytes accessed | tf_op | source)
XLA Modules:
  0.0 32.7 jit_solution(3465415239690103882)
XLA Ops:
  0.6 31.4 %translate.1.tiles = f32[192,128]{1,0:T(8,128)S(1)} custom-call(bf16[200,158]{1,0:T(8,128)(2,1)} %constant.2.clone.picks_hbm, bf16[4,4,8,64]{3,2,1,0:T(8,128)(2,1)} %fine_hbm.1, bf16[64,64,158]{2,1,0:T(8,128)(2,1)} %bitcast.2, bf16[4,4,4,64]{3,2,1,0:T(4,128)(2,1)} %coarse_hbm.1, bf16[64,64,158]{2,1,0:T(8,128)(2,1)} %bitcast.3), custom_call_target="tpu_custom_call" | custom-call | tf_op jit(solution)/shard_map/translate/pallas_call | solution.py:389
  32.0 0.7 %place.1 = (f32[4,4,8,64]{3,2,1,0:T(8,128)}, f32[4,4,4,64]{3,2,1,0:T(4,128)}) custom-call(f32[192,128]{1,0:T(8,128)S(1)} %translate.1.tiles), custom_call_target="tpu_custom_call" | custom-call | tf_op jit(solution)/shard_map/place/pallas_call | solution.py:434

commit v6 on v5

--- a/solution.py
+++ b/solution.py
@@ -352,7 +352,7 @@
     build_weights(turned, coarse_weights)
 
     use(OWN, own_copies)
-    answer(0, phase < 2)
+    answer(0, phase == 0)
     answer(1, phase == 3)
 
     @pl.loop(0, 2)
@@ -361,6 +361,7 @@
 
         @pl.when(above & in_y(1))
         def _():
+            answer(0, phase == 1)
             receive(1, ABOVE)
             use(ABOVE, share(ABOVE))
 

time: 32.9 us -> 36.5 us (1.11)
  the two profiles are of different devices: /device:TPU:256 before, /device:TPU:707 now
where the time goes in v6:
time: 36.5 us; the launch traced here: 36.4 us
  Pallas kernels  35.7 us (98%)
  between operations  0.64 us (2%)
    pallas_call x1, Pallas kernels, body(): pl.pallas_call(functools.partial(kernel, sizes), out_shape=pltpu.VMEM((19...  35 us

profile of v6, /device:TPU:707, one launch (start us, length us, event | category | flops | bytes accessed | tf_op | source)
XLA Modules:
  0.0 36.4 jit_solution(10784100816951228502)
XLA Ops:
  0.6 35.0 %translate.1.tiles = f32[192,128]{1,0:T(8,128)S(1)} custom-call(bf16[200,158]{1,0:T(8,128)(2,1)} %constant.2.clone.picks_hbm, bf16[4,4,8,64]{3,2,1,0:T(8,128)(2,1)} %fine_hbm.1, bf16[64,64,158]{2,1,0:T(8,128)(2,1)} %bitcast.2, bf16[4,4,4,64]{3,2,1,0:T(4,128)(2,1)} %coarse_hbm.1, bf16[64,64,158]{2,1,0:T(8,128)(2,1)} %bitcast.3), custom_call_target="tpu_custom_call" | custom-call | tf_op jit(solution)/shard_map/translate/pallas_call | solution.py:390
  35.7 0.7 %place.1 = (f32[4,4,8,64]{3,2,1,0:T(8,128)}, f32[4,4,4,64]{3,2,1,0:T(4,128)}) custom-call(f32[192,128]{1,0:T(8,128)S(1)} %translate.1.tiles), custom_call_target="tpu_custom_call" | custom-call | tf_op jit(solution)/shard_map/place/pallas_call | solution.py:435
